TPU v7x, 512 devices: a whole 4x8x8 slice. The times are simulated.
512 devices in a mesh: wide: 64 (over z_lo, y, core), narrow: 8 (over x, z_hi).
Axes of the slice: x: 4, y: 8, z: 8 (z_hi: 2, z_lo: 4; z = z_hi * 4 + z_lo), core: 2. Of those that a mesh axis runs over, the one named last changes fastest.
Arguments:
- features: bfloat16 [16, 1024, 2, 1024], P(None, 'wide', None, 'narrow'), may hold values from -6 to 6
- cotangent: bfloat16 [16, 1024, 2, 1024], P(None, 'wide', None, 'narrow'), may hold values from -6 to 6
- coarse_weight: bfloat16 [32, 16, 3, 3, 3], replicated, may hold values from -0.3125 to 0.3125
- fine_weight: bfloat16 [16, 48, 3, 3, 3], replicated, may hold values from -0.15625 to 0.15625
Outputs:
- output: bfloat16 [16, 1024, 2, 1024], P(None, 'wide', None, 'narrow')
- grad_features: bfloat16 [16, 1024, 2, 1024], P(None, 'wide', None, 'narrow')
- grad_fine: float32 [16, 48, 3, 3, 3], replicated
- grad_coarse: float32 [32, 16, 3, 3, 3], replicated
All inputs are finite; a program needn't handle non-finite values.
Results may differ from a plain program's by a relative error of at most 0.012.
Values may be sent and summed in bfloat16 or wider, within the bound.
A program may use at most 64 MiB of HBM per device.

v0:
```python
import math
import jax
import jax.numpy as jnp
from jax import lax
from jax.sharding import PartitionSpec as P


def extended_2(array, sides, width):
    for axis, dim in sides:
        count, length = (lax.axis_size(axis), array.shape[dim])
        up = [(i, (i + 1) % count) for i in range(count - 1)]
        down = [(j, i) for i, j in up]
        last = lax.slice_in_dim(array, length - width, length, axis=dim)
        first = lax.slice_in_dim(array, 0, width, axis=dim)
        before = lax.ppermute(last, axis, up)
        after = lax.ppermute(first, axis, down)
        array = jnp.concatenate([before, array, after], axis=dim)
    return array


def shortened(array):
    return jax.tree.map(lambda a: a.astype(jnp.bfloat16) if a.dtype == jnp.float32 else a, array)


def correlate(padded, kernel):
    result = lax.conv_general_dilated(
        padded[None],
        kernel,
        (1, 1, 1),
        "VALID",
        dimension_numbers=("NCHWD", "OIHWD", "NCHWD"),
        preferred_element_type=jnp.float32,
    )
    return result[0]


def weight_grad(padded, grad):
    result = lax.conv_general_dilated(
        padded[:, None],
        grad[:, None],
        (1, 1, 1),
        "VALID",
        dimension_numbers=("NCHWD", "OIHWD", "NCHWD"),
        preferred_element_type=jnp.float32,
    )
    return jnp.transpose(result, (1, 0, 2, 3, 4))


def flipped(kernel):
    return jnp.transpose(kernel[:, :, ::-1, ::-1, ::-1], (1, 0, 2, 3, 4))


def pool_sum(field):
    chans, rows, planes, cols = field.shape
    return field.reshape(chans, rows // 2, 2, planes // 2, 2, cols // 2, 2).sum(axis=(2, 4, 6))


def upsample(field):
    chans, rows, planes, cols = field.shape
    spread = jnp.broadcast_to(
        field[:, :, None, :, None, :, None], (chans, rows, 2, planes, 2, cols, 2)
    )
    return spread.reshape(chans, 2 * rows, 2 * planes, 2 * cols)


def silu_slope(value):
    sig = jax.nn.sigmoid(value)
    return sig * (1.0 + value * (1.0 - sig))


def fine_padded(field):
    extended = extended_2(field, (("wide", 1), ("narrow", 3)), 1)
    return jnp.pad(extended, ((0, 0), (0, 0), (1, 1), (0, 0)))


def coarse_padded(field):
    extended = extended_2(field, ((("wide", "narrow"), 1),), 1)
    return jnp.pad(extended, ((0, 0), (0, 0), (1, 1), (1, 1)))


def into_coarse(field):
    return jax.tree.map(
        lambda part, own: part.astype(own.dtype),
        lax.all_to_all(shortened(field), "narrow", split_axis=1, concat_axis=3, tiled=True),
        field,
    )


def into_fine(field):
    return jax.tree.map(
        lambda part, own: part.astype(own.dtype),
        lax.all_to_all(shortened(field), "narrow", split_axis=3, concat_axis=1, tiled=True),
        field,
    )


def shards(features, cotangent, coarse_weight, fine_weight):
    channels = features.shape[0]
    pooled = (pool_sum(features.astype(jnp.float32)) / 8.0).astype(jnp.bfloat16)
    coarse_ext = coarse_padded(into_coarse(pooled))
    coarse_pre = correlate(coarse_ext, coarse_weight)
    coarse_act = jax.nn.silu(coarse_pre).astype(jnp.bfloat16)
    upsampled = upsample(into_fine(coarse_act))
    joined_ext = fine_padded(jnp.concatenate([features, upsampled], 0))
    cotangent_ext = fine_padded(cotangent)
    output = correlate(joined_ext, fine_weight).astype(jnp.bfloat16)
    local_fine = weight_grad(joined_ext, cotangent)
    grad_joined = correlate(cotangent_ext, flipped(fine_weight))
    grad_act = into_coarse(pool_sum(grad_joined[channels:]).astype(jnp.bfloat16))
    grad_pre = (grad_act.astype(jnp.float32) * silu_slope(coarse_pre)).astype(jnp.bfloat16)
    local_coarse = weight_grad(coarse_ext, grad_pre)
    grad_pooled = correlate(coarse_padded(grad_pre), flipped(coarse_weight)).astype(jnp.bfloat16)
    grad_features = (
        grad_joined[:channels] + upsample(into_fine(grad_pooled)).astype(jnp.float32) / 8.0
    ).astype(jnp.bfloat16)
    fine_total, coarse_total = lax.psum((local_fine, local_coarse), ("wide", "narrow"))
    all_cells = (
        features.shape[1]
        * features.shape[2]
        * features.shape[3]
        * lax.axis_size("wide")
        * lax.axis_size("narrow")
    )
    return (
        output,
        grad_features,
        fine_total / math.sqrt(all_cells),
        coarse_total / math.sqrt(all_cells // 8),
    )


def solution(mesh):
    placed = (P(None, "wide", None, "narrow"), P(None, "wide", None, "narrow"), P(), P())
    return jax.shard_map(
        shards,
        mesh=mesh,
        in_specs=placed,
        out_specs=(P(None, "wide", None, "narrow"), P(None, "wide", None, "narrow"), P(), P()),
        check_vma=False,
    )
```

profile of v0, /device:TPU:1, one launch (start us, length us, event | category | flops | bytes accessed | tf_op | source)
XLA Modules:
  0.0 639.0 jit_solution(16950988302908629010)
XLA Ops:
  8.0 4.6 collective-permute-start.6
  12.6 5.5 collective-permute-start.7
  18.1 1.3 convert_reduce_fusion
  21.0 1.3 collective-permute-start.9
  22.3 8.1 %collective-permute-start.8 = (bf16[16,18,2,1]{3,2,1,0:T(2,128)(2,1)S(1)}, bf16[16,18,2,1]{3,2,1,0:T(2,128)(2,1)S(1)}, u32[]{:S(2)}, u32[]{:S(2)}) collective-permute-start(bf16[16,18,2,1]{3,2,1,0:T(2,128)(2,1)S(1)} %get-tuple-element.36), channel_id=1, source_target_pairs={{0,1},{1,2},{2,3},{3,4},{4,5},{5,6},{6,7},{8,9},{9,10},{10,11},{11... | collective-permute-start | bytes 3464 | tf_op jit(solution)/shard_map/ppermute | solution.py:15
  31.3 10.0 %all-to-all-start = ((bf16[8,2,512]{2,1,0:T(2,128)(2,1)}), bf16[8,2,512]{2,1,0:T(2,128)(2,1)S(1)}, u32[]{:S(2)}, u32[]{:S(2)}) async-start(bf16[8,2,512]{2,1,0:T(2,128)(2,1)} %reshape.289), calls=%async_computation | async-start | bytes 32768 | tf_op jit(solution)/shard_map/all_to_all | solution.py:84
  41.3 3.8 copy.231
  45.1 1.3 fusion.54
  46.7 1.8 reshape.286
  48.5 5.1 copy.219
  53.6 1.0 slice.64
  54.7 5.0 fusion.26
  60.4 2.0 copy.221
  62.6 8.5 %collective-permute-start.1 = (bf16[16,1,1,512]{3,0,2,1:T(8,128)(2,1)S(1)}, bf16[16,1,1,512]{3,0,2,1:T(8,128)(2,1)S(1)}, u32[]{:S(2)}, u32[]{:S(2)}) collective-permute-start(bf16[16,1,1,512]{3,0,2,1:T(8,128)(2,1)S(1)} %all_to_all.11), channel_id=1, source_target_pairs={{1,0},{2,1},{3,2},{4,3},{5,4},{6,5},{7,6},{8,7},{9,8},{10,9},{11,1... | collective-permute-start | bytes 49160 | tf_op jit(solution)/shard_map/ppermute | solution.py:16
  71.1 2.1 collective-permute-start
  73.2 1.9 slice_reduce_fusion
  75.1 1.8 reduce_sum.37
  78.6 10.8 %all-to-all-start.2 = ((bf16[8,2,1024]{2,1,0:T(2,128)(2,1)}), bf16[8,2,1024]{2,1,0:T(2,128)(2,1)S(1)}, u32[]{:S(2)}, u32[]{:S(2)}) async-start(bf16[8,2,1024]{2,1,0:T(2,128)(2,1)} %reshape.287), calls=%async_computation.2 | async-start | bytes 65536 | tf_op jit(solution)/shard_map/all_to_all | solution.py:84
  89.4 2.8 copy.220
  92.2 2.8 reshape.252
  97.0 1.2 fusion.46
  99.3 2.0 copy.233
  101.6 8.2 %collective-permute-start.11 = (bf16[32,1,1,512]{3,0,2,1:T(8,128)(2,1)S(1)}, bf16[32,1,1,512]{3,0,2,1:T(8,128)(2,1)S(1)}, u32[]{:S(2)}, u32[]{:S(2)}) collective-permute-start(bf16[32,1,1,512]{3,0,2,1:T(8,128)(2,1)S(1)} %get-tuple-element.40), channel_id=1, source_target_pairs={{1,0},{2,1},{3,2},{4,3},{5,4},{6,5},{7,6},{8,7},{9,8},{10,9},{11,1... | collective-permute-start | bytes 98312 | tf_op jit(solution)/shard_map/ppermute | solution.py:16
  109.7 1.9 collective-permute-start.10
  112.4 1.5 reduce.8
  114.7 11.2 %all-to-all-start.1 = ((bf16[8,2,1024]{2,1,0:T(2,128)(2,1)}), bf16[8,2,1024]{2,1,0:T(2,128)(2,1)S(1)}, u32[]{:S(2)}, u32[]{:S(2)}) async-start(bf16[8,2,1024]{2,1,0:T(2,128)(2,1)} %reshape.291), calls=%async_computation.1 | async-start | bytes 65536 | tf_op jit(solution)/shard_map/all_to_all | solution.py:92
  126.1 5.7 fusion.101
  131.8 105.8 %psum.15 = f32[32,16,3,3,3]{0,1,4,3,2:T(8,128)S(1)} all-reduce(f32[32,16,3,3,3]{0,1,4,3,2:T(8,128)S(1)} %fusion.101), channel_id=1, replica_groups=mesh['wide'=64,'narrow'=8] {'wide','narrow'}, use_global_device_ids=true, to_apply=%region_5.6 | all-reduce | flops 13824 | bytes 110592 | tf_op jit(solution)/shard_map/psum | solution.py:116
  239.0 1.7 copy.225
  240.8 1.1 fusion.33
  242.3 1.5 reduce.9
  244.6 3.3 all-to-all-start.3
  248.9 2.9 collective-permute-start.3
  251.8 2.6 collective-permute-start.2
  254.4 2.4 all-to-all-done.3
  258.3 1.3 collective-permute-start.5
  259.6 8.3 %collective-permute-start.4 = (bf16[48,18,2,1]{3,0,2,1:T(8,128)(2,1)S(1)}, bf16[48,18,2,1]{3,0,2,1:T(8,128)(2,1)S(1)}, u32[]{:S(2)}, u32[]{:S(2)}) collective-permute-start(bf16[48,18,2,1]{3,0,2,1:T(8,128)(2,1)S(1)} %get-tuple-element.32), channel_id=1, source_target_pairs={{0,1},{1,2},{2,3},{3,4},{4,5},{5,6},{6,7},{8,9},{9,10},{10,11},{11... | collective-permute-start | bytes 10376 | tf_op jit(solution)/shard_map/ppermute | solution.py:15
  268.7 5.5 collective-permute-done.5
  275.9 2.0 fusion.111
  277.9 4.9 copy.240
  282.8 1.3 pad.22.clone
  284.5 6.5 %fusion.9 = bf16[16,2,8,17,16]{4,2,3,1,0:T(8,128)(2,1)} fusion(bf16[16,48,3,3,3]{1,0,4,3,2:T(8,128)(2,1)S(1)} %copy-done, bf16[48,18,4,1,7,2]{0,4,5,2,1,3:T(8,128)(2,1)S(1)} %slice.60, bf16[48,18,4,1,8,17]{0,4,5,2,1,3:T(8,128)(2,1)S(1)} %copy.213), kind=kOutput, calls=%fused_computation.12 | convolution fusion | flops 183638016 | bytes 1217536 | tf_op jit(solution)/shard_map/conv_general_dilated | solution.py:26
  291.0 2.7 copy.214
  295.1 1.1 fusion.110
  296.2 8.8 %copy.230 = bf16[48,1,18,4,130]{0,1,4,3,2:T(2,128)(2,1)} copy(bf16[48,1,18,4,130]{4,0,3,2,1:T(8,128)(2,1)S(1)} %fusion.110) | data formatting | bytes 1797120 | tf_op jit(solution)/shard_map/broadcast_in_dim | solution.py:39
  305.0 31.3 %fusion.100 = f32[16,48,3,3,3]{1,0,4,3,2:T(8,128)} fusion(bf16[48,1,18,4,130]{0,1,4,3,2:T(2,128)(2,1)} %copy.230, bf16[16,1,16,2,128]{0,1,4,3,2:T(2,128)(2,1)} %copy.231), kind=kOutput, calls=%fused_computation.139 | convolution fusion | flops 169869312 | bytes 1112576 | tf_op jit(solution)/shard_map/transpose | solution.py:46
  337.1 293.2 %all-reduce.6.cloned.1.call-done = f32[16,48,3,3,3]{1,0,4,3,2:T(8,128)} async-done(((f32[16,48,3,3,3]{1,0,4,3,2:T(8,128)}), f32[16,48,3,3,3]{1,0,4,3,2:T(8,128)}) %all-reduce.6.cloned.1.call-update) | async-done | bytes 82960 | tf_op jit(solution)/shard_map/psum | solution.py:116
  630.3 1.6 broadcast_multiply_fusion.1
  (107 shorter events, 21.2 us)
Async XLA Ops:
  7.2 47.5 %copy-start = (bf16[16,48,3,3,3]{1,0,4,3,2:T(8,128)(2,1)S(1)}, bf16[16,48,3,3,3]{1,0,4,3,2:T(8,128)(2,1)}, u32[]{:S(2)}) copy-start(bf16[16,48,3,3,3]{1,0,4,3,2:T(8,128)(2,1)} %param.7) | copy-start | bytes 124420
  7.2 13.4 %copy-start.4 = (bf16[16,16,2,128]{3,2,1,0:T(2,128)(2,1)S(1)}, bf16[16,16,2,128]{3,2,1,0:T(2,128)(2,1)}, u32[]{:S(2)}) copy-start(bf16[16,16,2,128]{3,2,1,0:T(2,128)(2,1)} %param.5) | copy-start | bytes 393220
  7.2 34.1 %copy-start.5 = (bf16[16,16,2,128]{3,2,1,0:T(2,128)(2,1)S(1)}, bf16[16,16,2,128]{3,2,1,0:T(2,128)(2,1)}, u32[]{:S(2)}) copy-start(bf16[16,16,2,128]{3,2,1,0:T(2,128)(2,1)} %param.4) | copy-start | bytes 393220
  8.0 12.6 %collective-permute-start.6 = (bf16[16,1,2,128]{3,2,1,0:T(2,128)(2,1)S(1)}, bf16[16,1,2,128]{3,2,1,0:T(2,128)(2,1)S(1)}, u32[]{:S(2)}, u32[]{:S(2)}) collective-permute-start(bf16[16,1,2,128]{3,2,1,0:T(2,128)(2,1)S(1)} %get-tuple-element.39), channel_id=1, source_target_pairs={{0,8},{8,16},{16,24},{24,32},{32,40},{40,48},{48,56},{56,64},{64,7... | collective-permute-start | bytes 24584 | tf_op jit(solution)/shard_map/ppermute | solution.py:15
  12.6 8.1 %collective-permute-start.7 = (bf16[16,1,2,128]{3,2,1,0:T(2,128)(2,1)S(1)}, bf16[16,1,2,128]{3,2,1,0:T(2,128)(2,1)S(1)}, u32[]{:S(2)}, u32[]{:S(2)}) collective-permute-start(bf16[16,1,2,128]{3,2,1,0:T(2,128)(2,1)S(1)} %get-tuple-element.38), channel_id=1, source_target_pairs={{8,0},{16,8},{24,16},{32,24},{40,32},{48,40},{56,48},{64,56},{72,6... | collective-permute-start | bytes 24584 | tf_op jit(solution)/shard_map/ppermute | solution.py:16
  21.0 24.1 %collective-permute-start.9 = (bf16[16,18,2,1]{3,2,1,0:T(2,128)(2,1)S(1)}, bf16[16,18,2,1]{3,2,1,0:T(2,128)(2,1)S(1)}, u32[]{:S(2)}, u32[]{:S(2)}) collective-permute-start(bf16[16,18,2,1]{3,2,1,0:T(2,128)(2,1)S(1)} %get-tuple-element.37), channel_id=1, source_target_pairs={{1,0},{2,1},{3,2},{4,3},{5,4},{6,5},{7,6},{9,8},{10,9},{11,10},{12... | collective-permute-start | bytes 3464 | tf_op jit(solution)/shard_map/ppermute | solution.py:16
  22.3 22.8 %collective-permute-start.8 = (bf16[16,18,2,1]{3,2,1,0:T(2,128)(2,1)S(1)}, bf16[16,18,2,1]{3,2,1,0:T(2,128)(2,1)S(1)}, u32[]{:S(2)}, u32[]{:S(2)}) collective-permute-start(bf16[16,18,2,1]{3,2,1,0:T(2,128)(2,1)S(1)} %get-tuple-element.36), channel_id=1, source_target_pairs={{0,1},{1,2},{2,3},{3,4},{4,5},{5,6},{6,7},{8,9},{9,10},{10,11},{11... | collective-permute-start | bytes 3464 | tf_op jit(solution)/shard_map/ppermute | solution.py:15
  31.3 31.1 %all-to-all-start = ((bf16[8,2,512]{2,1,0:T(2,128)(2,1)}), bf16[8,2,512]{2,1,0:T(2,128)(2,1)S(1)}, u32[]{:S(2)}, u32[]{:S(2)}) async-start(bf16[8,2,512]{2,1,0:T(2,128)(2,1)} %reshape.289), calls=%async_computation | async-start | bytes 32768 | tf_op jit(solution)/shard_map/all_to_all | solution.py:84
  48.5 6.2 copy-start.10
  62.6 32.4 %collective-permute-start.1 = (bf16[16,1,1,512]{3,0,2,1:T(8,128)(2,1)S(1)}, bf16[16,1,1,512]{3,0,2,1:T(8,128)(2,1)S(1)}, u32[]{:S(2)}, u32[]{:S(2)}) collective-permute-start(bf16[16,1,1,512]{3,0,2,1:T(8,128)(2,1)S(1)} %all_to_all.11), channel_id=1, source_target_pairs={{1,0},{2,1},{3,2},{4,3},{5,4},{6,5},{7,6},{8,7},{9,8},{10,9},{11,1... | collective-permute-start | bytes 49160 | tf_op jit(solution)/shard_map/ppermute | solution.py:16
  71.1 23.9 %collective-permute-start = (bf16[16,1,1,512]{3,0,2,1:T(8,128)(2,1)S(1)}, bf16[16,1,1,512]{3,0,2,1:T(8,128)(2,1)}, u32[]{:S(2)}, u32[]{:S(2)}) collective-permute-start(bf16[16,1,1,512]{3,0,2,1:T(8,128)(2,1)S(1)} %all_to_all.11), channel_id=1, source_target_pairs={{0,1},{1,2},{2,3},{3,4},{4,5},{5,6},{6,7},{7,8},{8,9},{9,10},{10,1... | collective-permute-start | bytes 49160 | tf_op jit(solution)/shard_map/ppermute | solution.py:15
  78.6 22.7 %all-to-all-start.2 = ((bf16[8,2,1024]{2,1,0:T(2,128)(2,1)}), bf16[8,2,1024]{2,1,0:T(2,128)(2,1)S(1)}, u32[]{:S(2)}, u32[]{:S(2)}) async-start(bf16[8,2,1024]{2,1,0:T(2,128)(2,1)} %reshape.287), calls=%async_computation.2 | async-start | bytes 65536 | tf_op jit(solution)/shard_map/all_to_all | solution.py:84
  92.2 4.7 copy-start.8
  92.2 4.7 copy-start.9
  101.6 136.7 %collective-permute-start.11 = (bf16[32,1,1,512]{3,0,2,1:T(8,128)(2,1)S(1)}, bf16[32,1,1,512]{3,0,2,1:T(8,128)(2,1)S(1)}, u32[]{:S(2)}, u32[]{:S(2)}) collective-permute-start(bf16[32,1,1,512]{3,0,2,1:T(8,128)(2,1)S(1)} %get-tuple-element.40), channel_id=1, source_target_pairs={{1,0},{2,1},{3,2},{4,3},{5,4},{6,5},{7,6},{8,7},{9,8},{10,9},{11,1... | collective-permute-start | bytes 98312 | tf_op jit(solution)/shard_map/ppermute | solution.py:16
  109.7 128.6 %collective-permute-start.10 = (bf16[32,1,1,512]{3,0,2,1:T(8,128)(2,1)S(1)}, bf16[32,1,1,512]{3,0,2,1:T(8,128)(2,1)S(1)}, u32[]{:S(2)}, u32[]{:S(2)}) collective-permute-start(bf16[32,1,1,512]{3,0,2,1:T(8,128)(2,1)S(1)} %get-tuple-element.40), channel_id=1, source_target_pairs={{0,1},{1,2},{2,3},{3,4},{4,5},{5,6},{6,7},{7,8},{8,9},{9,10},{10,1... | collective-permute-start | bytes 98312 | tf_op jit(solution)/shard_map/ppermute | solution.py:15
  114.7 129.9 %all-to-all-start.1 = ((bf16[8,2,1024]{2,1,0:T(2,128)(2,1)}), bf16[8,2,1024]{2,1,0:T(2,128)(2,1)S(1)}, u32[]{:S(2)}, u32[]{:S(2)}) async-start(bf16[8,2,1024]{2,1,0:T(2,128)(2,1)} %reshape.291), calls=%async_computation.1 | async-start | bytes 65536 | tf_op jit(solution)/shard_map/all_to_all | solution.py:92
  240.7 1.3 copy-start.7
  244.6 12.2 %all-to-all-start.3 = ((bf16[8,2,512]{2,1,0:T(2,128)(2,1)}), bf16[8,2,512]{2,1,0:T(2,128)(2,1)S(1)}, u32[]{:S(2)}, u32[]{:S(2)}) async-start(bf16[8,2,512]{2,1,0:T(2,128)(2,1)} %reshape.293), calls=%async_computation.3 | async-start | bytes 32768 | tf_op jit(solution)/shard_map/all_to_all | solution.py:92
  247.9 382.4 %all-reduce.6.cloned.1.call-start = ((), (), s32[]{:S(2)}) async-start(), calls=%async_computation.4 | async-start | bytes 442368 | tf_op jit(solution)/shard_map/psum | solution.py:116
  248.9 9.2 %collective-permute-start.3 = (bf16[48,1,2,128]{3,0,2,1:T(8,128)(2,1)S(1)}, bf16[48,1,2,128]{3,0,2,1:T(8,128)(2,1)S(1)}, u32[]{:S(2)}, u32[]{:S(2)}) collective-permute-start(bf16[48,1,2,128]{3,0,2,1:T(8,128)(2,1)S(1)} %get-tuple-element.35), channel_id=1, source_target_pairs={{8,0},{16,8},{24,16},{32,24},{40,32},{48,40},{56,48},{64,56},{72,6... | collective-permute-start | bytes 73736 | tf_op jit(solution)/shard_map/ppermute | solution.py:16
  251.8 6.3 collective-permute-start.2
  257.3 10.6 %copy-start.3 = (f32[16,2,1,136,16]{3,4,1,0,2:T(8,128)S(1)}, f32[16,2,1,136,16]{3,4,1,0,2:T(8,128)}, u32[]{:S(2)}) copy-start(f32[16,2,1,136,16]{3,4,1,0,2:T(8,128)} %reshape.252) | copy-start | bytes 835588
  258.3 15.9 %collective-permute-start.5 = (bf16[48,18,2,1]{3,0,2,1:T(8,128)(2,1)S(1)}, bf16[48,18,2,1]{3,0,2,1:T(8,128)(2,1)S(1)}, u32[]{:S(2)}, u32[]{:S(2)}) collective-permute-start(bf16[48,18,2,1]{3,0,2,1:T(8,128)(2,1)S(1)} %get-tuple-element.33), channel_id=1, source_target_pairs={{1,0},{2,1},{3,2},{4,3},{5,4},{6,5},{7,6},{9,8},{10,9},{11,10},{12... | collective-permute-start | bytes 10376 | tf_op jit(solution)/shard_map/ppermute | solution.py:16
  259.6 15.6 %collective-permute-start.4 = (bf16[48,18,2,1]{3,0,2,1:T(8,128)(2,1)S(1)}, bf16[48,18,2,1]{3,0,2,1:T(8,128)(2,1)S(1)}, u32[]{:S(2)}, u32[]{:S(2)}) collective-permute-start(bf16[48,18,2,1]{3,0,2,1:T(8,128)(2,1)S(1)} %get-tuple-element.32), channel_id=1, source_target_pairs={{0,1},{1,2},{2,3},{3,4},{4,5},{5,6},{6,7},{8,9},{9,10},{10,11},{11... | collective-permute-start | bytes 10376 | tf_op jit(solution)/shard_map/ppermute | solution.py:15
  275.2 0.8 copy-start.1
  284.5 9.3 %copy-start.6 = (pred[8,17]{1,0:T(8,128)(4,1)S(1)}, pred[8,17]{1,0:T(8,128)(4,1)}, u32[]{:S(2)}) copy-start(pred[8,17]{1,0:T(8,128)(4,1)} %constant.46) | copy-start | bytes 412
  293.8 1.3 copy-start.2
Sparse Core Ops, SparseCore 0:
  336.4 293.8 all-reduce.5
where the time goes:
time: 648 us; the launch traced here: 639 us
  waiting for transfers between devices  302 us (47%)
  blocking collectives  106 us (16%)
  starting transfers between devices  90.7 us (14%)
  local copies, waits for them, and re-layouts  56.7 us (9%)
  matrix products  50.9 us (8%)
  other arithmetic  18 us (3%)
  between operations  14.9 us (2%)
    psum x1, waiting for transfers between devices, shards(): lax.psum((local_fine, local_coarse), ('wide', 'narrow'))  293 us
    psum x1, blocking collectives, shards(): lax.psum((local_fine, local_coarse), ('wide', 'narrow'))  106 us
    transpose x2, matrix products, weight_grad(): return jnp.transpose(result, (1, 0, 2, 3, 4))  37 us
    ppermute x6, starting transfers between devices, extended_2(): before = lax.ppermute(last, axis, up)  27.7 us
    ppermute x6, starting transfers between devices, extended_2(): after = lax.ppermute(first, axis, down)  27.6 us
    conv_general_dilated x19, local copies, waits for them, and re-layouts, correlate(): lax.conv_general_dilated(padded[None], kernel, (1, 1, 1), 'VALID', dimens...  23.1 us
    all_to_all x2, starting transfers between devices, into_coarse(): lax.all_to_all(shortened(field), 'narrow', split_axis=1, concat_axis=3, t...  20.8 us
    all_to_all x2, starting transfers between devices, into_fine(): lax.all_to_all(shortened(field), 'narrow', split_axis=3, concat_axis=1, t...  14.5 us
  transfers between devices with their start and end apart: 17, of which 4 were waited for; matrix products, arithmetic and copies ran while one was open for 10% of the time, Pallas kernels for 0%

commit v1 on v0

--- a/solution.py
+++ b/solution.py
@@ -1,8 +1,18 @@
+import functools
 import math
 import jax
 import jax.numpy as jnp
 from jax import lax
 from jax.sharding import PartitionSpec as P
+
+
+def group_the_values(body, mesh_dim, axis_key):
+    for tick in (mesh_dim, axis_key):
+        body = lax.psum(body, tick)
+    return body
+
+
+obtain_digits = functools.partial(group_the_values, mesh_dim="narrow", axis_key="wide")
 
 
 def extended_2(array, sides, width):
@@ -113,7 +123,7 @@
     grad_features = (
         grad_joined[:channels] + upsample(into_fine(grad_pooled)).astype(jnp.float32) / 8.0
     ).astype(jnp.bfloat16)
-    fine_total, coarse_total = lax.psum((local_fine, local_coarse), ("wide", "narrow"))
+    fine_total, coarse_total = obtain_digits((local_fine, local_coarse))
     all_cells = (
         features.shape[1]
         * features.shape[2]

time: 648 us -> 1190 us (1.84)
  waiting for transfers between devices: 302 us -> 606 us
  blocking collectives: 106 us -> 330 us
    psum x1 -> x2, waiting for transfers between devices: 293 us -> 602 us  [group_the_values(): body = lax.psum(body, tick)]
    psum x1 -> x2, blocking collectives: 106 us -> 330 us  [group_the_values(): body = lax.psum(body, tick)]
  transfers between devices with their start and end apart: 17 -> 18, of which waited for: 4 -> 4; matrix products, arithmetic and copies ran while one was open for 10% -> 6% of each run, Pallas kernels for 0% -> 0%
where the time goes in v1:
time: 1190 us; the launch traced here: 1180 us
  waiting for transfers between devices  606 us (51%)
  blocking collectives  330 us (28%)
  starting transfers between devices  95.2 us (8%)
  local copies, waits for them, and re-layouts  58.4 us (5%)
  matrix products  51.6 us (4%)
  other arithmetic  21.1 us (2%)
  between operations  15.1 us (1%)
    psum x2, waiting for transfers between devices, group_the_values(): body = lax.psum(body, tick)  602 us
    psum x2, blocking collectives, group_the_values(): body = lax.psum(body, tick)  330 us
    transpose x2, matrix products, weight_grad(): return jnp.transpose(result, (1, 0, 2, 3, 4))  37.7 us
    ppermute x6, starting transfers between devices, extended_2(): after = lax.ppermute(first, axis, down)  33 us
    ppermute x6, starting transfers between devices, extended_2(): before = lax.ppermute(last, axis, up)  26.8 us
  transfers between devices with their start and end apart: 18, of which 4 were waited for; matrix products, arithmetic and copies ran while one was open for 6% of the time, Pallas kernels for 0%

profile of v1, /device:TPU:1, one launch (start us, length us, event | category | flops | bytes accessed | tf_op | source)
XLA Modules:
  0.0 1177.9 jit_solution(5425676697788141247)
XLA Ops:
  8.0 4.6 collective-permute-start.6
  12.6 5.5 collective-permute-start.7
  18.1 1.3 convert_reduce_fusion
  21.0 1.3 collective-permute-start.9
  22.3 8.1 collective-permute-start.8
  31.3 10.0 all-to-all-start
  41.3 3.8 copy.231
  45.1 1.3 fusion.54
  46.7 1.8 reshape.286
  48.6 5.0 copy.219
  54.7 5.0 fusion.26
  60.3 2.0 copy.221
  62.6 8.5 collective-permute-start.1
  71.1 2.2 collective-permute-start
  73.3 1.9 slice_reduce_fusion
  75.2 1.8 reduce_sum.37
  78.7 10.8 all-to-all-start.2
  89.5 2.8 copy.220
  92.3 2.1 reshape.252
  98.7 2.0 copy.233
  101.0 8.2 collective-permute-start.11
  109.2 1.9 collective-permute-start.10
  112.5 2.1 reduce.8
  114.6 1.7 reshape.291
  116.3 11.2 all-to-all-start.1
  128.5 6.4 fusion.101
  134.9 53.1 %psum.30 = f32[32,16,3,3,3]{0,1,4,3,2:T(8,128)S(1)} all-reduce(f32[32,16,3,3,3]{0,1,4,3,2:T(8,128)} %fusion.101), channel_id=1, replica_groups=mesh['wide'=64,'narrow'=8] {'narrow'}, use_global_device_ids=true, to_apply=%region_6.7 | all-reduce | flops 13824 | bytes 110592 | tf_op jit(solution)/shard_map/psum | solution.py:11
  188.0 277.0 %psum.31 = f32[32,16,3,3,3]{0,1,4,3,2:T(8,128)S(1)} all-reduce(f32[32,16,3,3,3]{0,1,4,3,2:T(8,128)S(1)} %psum.30), channel_id=1, replica_groups=mesh['wide'=64,'narrow'=8] {'wide'}, use_global_device_ids=true, to_apply=%region_7.8 | all-reduce | flops 13824 | bytes 110592 | tf_op jit(solution)/shard_map/psum | solution.py:11
  467.2 1.7 copy.225
  470.5 1.4 reduce.9
  472.7 3.3 all-to-all-start.3
  477.7 8.3 collective-permute-start.3
  486.0 1.9 collective-permute-start.2
  489.4 1.3 collective-permute-start.5
  490.7 8.1 collective-permute-start.4
  499.5 2.9 collective-permute-done.5
  502.5 1.5 collective-permute-done.4
  504.7 2.0 fusion.111
  506.7 4.9 copy.240
  511.6 1.3 pad.22.clone
  513.3 6.5 fusion.9
  519.8 2.7 copy.214
  522.6 2.1 fusion.110
  524.7 8.8 copy.230
  533.6 31.3 %fusion.100 = f32[16,48,3,3,3]{1,0,4,3,2:T(8,128)} fusion(bf16[48,1,18,4,130]{0,1,4,3,2:T(2,128)(2,1)} %copy.230, bf16[16,1,16,2,128]{0,1,4,3,2:T(2,128)(2,1)} %copy.231), kind=kOutput, calls=%fused_computation.139 | convolution fusion | flops 169869312 | bytes 1112576 | tf_op jit(solution)/shard_map/transpose | solution.py:56
  566.3 114.6 %all-reduce.7.cloned.1.call-done = f32[16,48,3,3,3]{1,0,4,3,2:T(8,128)} async-done(((f32[16,48,3,3,3]{1,0,4,3,2:T(8,128)}), f32[16,48,3,3,3]{1,0,4,3,2:T(8,128)}) %all-reduce.7.cloned.1.call-update) | async-done | bytes 82960 | tf_op jit(solution)/shard_map/psum | solution.py:11
  681.7 487.3 %all-reduce.9.cloned.1.call-done = f32[16,48,3,3,3]{1,0,4,3,2:T(8,128)} async-done(((f32[16,48,3,3,3]{1,0,4,3,2:T(8,128)}), f32[16,48,3,3,3]{1,0,4,3,2:T(8,128)}) %all-reduce.9.cloned.1.call-update) | async-done | bytes 82960 | tf_op jit(solution)/shard_map/psum | solution.py:11
  1169.0 1.6 broadcast_multiply_fusion.1
  (111 shorter events, 25.9 us)
Async XLA Ops:
  7.2 47.5 %copy-start = (bf16[16,48,3,3,3]{1,0,4,3,2:T(8,128)(2,1)S(1)}, bf16[16,48,3,3,3]{1,0,4,3,2:T(8,128)(2,1)}, u32[]{:S(2)}) copy-start(bf16[16,48,3,3,3]{1,0,4,3,2:T(8,128)(2,1)} %param.7) | copy-start | bytes 124420
  7.2 13.4 %copy-start.3 = (bf16[16,16,2,128]{3,2,1,0:T(2,128)(2,1)S(1)}, bf16[16,16,2,128]{3,2,1,0:T(2,128)(2,1)}, u32[]{:S(2)}) copy-start(bf16[16,16,2,128]{3,2,1,0:T(2,128)(2,1)} %param.5) | copy-start | bytes 393220
  7.2 34.1 %copy-start.4 = (bf16[16,16,2,128]{3,2,1,0:T(2,128)(2,1)S(1)}, bf16[16,16,2,128]{3,2,1,0:T(2,128)(2,1)}, u32[]{:S(2)}) copy-start(bf16[16,16,2,128]{3,2,1,0:T(2,128)(2,1)} %param.4) | copy-start | bytes 393220
  8.0 12.6 %collective-permute-start.6 = (bf16[16,1,2,128]{3,2,1,0:T(2,128)(2,1)S(1)}, bf16[16,1,2,128]{3,2,1,0:T(2,128)(2,1)S(1)}, u32[]{:S(2)}, u32[]{:S(2)}) collective-permute-start(bf16[16,1,2,128]{3,2,1,0:T(2,128)(2,1)S(1)} %get-tuple-element.39), channel_id=1, source_target_pairs={{0,8},{8,16},{16,24},{24,32},{32,40},{40,48},{48,56},{56,64},{64,7... | collective-permute-start | bytes 24584 | tf_op jit(solution)/shard_map/ppermute | solution.py:25
  12.6 8.1 collective-permute-start.7
  21.0 24.1 %collective-permute-start.9 = (bf16[16,18,2,1]{3,2,1,0:T(2,128)(2,1)S(1)}, bf16[16,18,2,1]{3,2,1,0:T(2,128)(2,1)S(1)}, u32[]{:S(2)}, u32[]{:S(2)}) collective-permute-start(bf16[16,18,2,1]{3,2,1,0:T(2,128)(2,1)S(1)} %get-tuple-element.37), channel_id=1, source_target_pairs={{1,0},{2,1},{3,2},{4,3},{5,4},{6,5},{7,6},{9,8},{10,9},{11,10},{12... | collective-permute-start | bytes 3464 | tf_op jit(solution)/shard_map/ppermute | solution.py:26
  22.3 22.8 %collective-permute-start.8 = (bf16[16,18,2,1]{3,2,1,0:T(2,128)(2,1)S(1)}, bf16[16,18,2,1]{3,2,1,0:T(2,128)(2,1)S(1)}, u32[]{:S(2)}, u32[]{:S(2)}) collective-permute-start(bf16[16,18,2,1]{3,2,1,0:T(2,128)(2,1)S(1)} %get-tuple-element.36), channel_id=1, source_target_pairs={{0,1},{1,2},{2,3},{3,4},{4,5},{5,6},{6,7},{8,9},{9,10},{10,11},{11... | collective-permute-start | bytes 3464 | tf_op jit(solution)/shard_map/ppermute | solution.py:25
  31.3 31.1 %all-to-all-start = ((bf16[8,2,512]{2,1,0:T(2,128)(2,1)}), bf16[8,2,512]{2,1,0:T(2,128)(2,1)S(1)}, u32[]{:S(2)}, u32[]{:S(2)}) async-start(bf16[8,2,512]{2,1,0:T(2,128)(2,1)} %reshape.289), calls=%async_computation | async-start | bytes 32768 | tf_op jit(solution)/shard_map/all_to_all | solution.py:94
  48.5 6.1 copy-start.10
  62.6 31.9 %collective-permute-start.1 = (bf16[16,1,1,512]{3,0,2,1:T(8,128)(2,1)S(1)}, bf16[16,1,1,512]{3,0,2,1:T(8,128)(2,1)S(1)}, u32[]{:S(2)}, u32[]{:S(2)}) collective-permute-start(bf16[16,1,1,512]{3,0,2,1:T(8,128)(2,1)S(1)} %all_to_all.11), channel_id=1, source_target_pairs={{1,0},{2,1},{3,2},{4,3},{5,4},{6,5},{7,6},{8,7},{9,8},{10,9},{11,1... | collective-permute-start | bytes 49160 | tf_op jit(solution)/shard_map/ppermute | solution.py:26
  71.1 23.4 %collective-permute-start = (bf16[16,1,1,512]{3,0,2,1:T(8,128)(2,1)S(1)}, bf16[16,1,1,512]{3,0,2,1:T(8,128)(2,1)}, u32[]{:S(2)}, u32[]{:S(2)}) collective-permute-start(bf16[16,1,1,512]{3,0,2,1:T(8,128)(2,1)S(1)} %all_to_all.11), channel_id=1, source_target_pairs={{0,1},{1,2},{2,3},{3,4},{4,5},{5,6},{6,7},{7,8},{8,9},{9,10},{10,1... | collective-permute-start | bytes 49160 | tf_op jit(solution)/shard_map/ppermute | solution.py:25
  78.7 22.1 %all-to-all-start.2 = ((bf16[8,2,1024]{2,1,0:T(2,128)(2,1)}), bf16[8,2,1024]{2,1,0:T(2,128)(2,1)S(1)}, u32[]{:S(2)}, u32[]{:S(2)}) async-start(bf16[8,2,1024]{2,1,0:T(2,128)(2,1)} %reshape.287), calls=%async_computation.2 | async-start | bytes 65536 | tf_op jit(solution)/shard_map/all_to_all | solution.py:94
  92.3 4.1 copy-start.7
  92.3 4.1 copy-start.9
  101.0 364.6 %collective-permute-start.11 = (bf16[32,1,1,512]{3,0,2,1:T(8,128)(2,1)S(1)}, bf16[32,1,1,512]{3,0,2,1:T(8,128)(2,1)}, u32[]{:S(2)}, u32[]{:S(2)}) collective-permute-start(bf16[32,1,1,512]{3,0,2,1:T(8,128)(2,1)S(1)} %get-tuple-element.40), channel_id=1, source_target_pairs={{1,0},{2,1},{3,2},{4,3},{5,4},{6,5},{7,6},{8,7},{9,8},{10,9},{11,1... | collective-permute-start | bytes 98312 | tf_op jit(solution)/shard_map/ppermute | solution.py:26
  109.2 356.5 %collective-permute-start.10 = (bf16[32,1,1,512]{3,0,2,1:T(8,128)(2,1)S(1)}, bf16[32,1,1,512]{3,0,2,1:T(8,128)(2,1)}, u32[]{:S(2)}, u32[]{:S(2)}) collective-permute-start(bf16[32,1,1,512]{3,0,2,1:T(8,128)(2,1)S(1)} %get-tuple-element.40), channel_id=1, source_target_pairs={{0,1},{1,2},{2,3},{3,4},{4,5},{5,6},{6,7},{7,8},{8,9},{9,10},{10,1... | collective-permute-start | bytes 98312 | tf_op jit(solution)/shard_map/ppermute | solution.py:25
  116.3 356.4 %all-to-all-start.1 = ((bf16[8,2,1024]{2,1,0:T(2,128)(2,1)}), bf16[8,2,1024]{2,1,0:T(2,128)(2,1)}, u32[]{:S(2)}, u32[]{:S(2)}) async-start(bf16[8,2,1024]{2,1,0:T(2,128)(2,1)} %reshape.291), calls=%async_computation.1 | async-start | bytes 65536 | tf_op jit(solution)/shard_map/all_to_all | solution.py:102
  188.0 280.9 %copy-start.8 = (bf16[32,16,3,3,3]{0,1,4,3,2:T(8,128)(2,1)S(1)}, bf16[32,16,3,3,3]{0,1,4,3,2:T(8,128)(2,1)}, u32[]{:S(2)}) copy-start(bf16[32,16,3,3,3]{0,1,4,3,2:T(8,128)(2,1)} %param.6) | copy-start | bytes 82948
  468.9 1.3 copy-start.6
  472.7 15.3 %all-to-all-start.3 = ((bf16[8,2,512]{2,1,0:T(2,128)(2,1)}), bf16[8,2,512]{2,1,0:T(2,128)(2,1)S(1)}, u32[]{:S(2)}, u32[]{:S(2)}) async-start(bf16[8,2,512]{2,1,0:T(2,128)(2,1)} %reshape.293), calls=%async_computation.3 | async-start | bytes 32768 | tf_op jit(solution)/shard_map/all_to_all | solution.py:102
  476.0 204.9 %all-reduce.7.cloned.1.call-start = ((), (), s32[]{:S(2)}) async-start(), calls=%async_computation.4 | async-start | bytes 442368 | tf_op jit(solution)/shard_map/psum | solution.py:11
  477.7 11.4 collective-permute-start.3
  486.0 3.2 collective-permute-start.2
  489.4 13.1 %collective-permute-start.5 = (bf16[48,18,2,1]{3,0,2,1:T(8,128)(2,1)S(1)}, bf16[48,18,2,1]{3,0,2,1:T(8,128)(2,1)S(1)}, u32[]{:S(2)}, u32[]{:S(2)}) collective-permute-start(bf16[48,18,2,1]{3,0,2,1:T(8,128)(2,1)S(1)} %get-tuple-element.33), channel_id=1, source_target_pairs={{1,0},{2,1},{3,2},{4,3},{5,4},{6,5},{7,6},{9,8},{10,9},{11,10},{12... | collective-permute-start | bytes 10376 | tf_op jit(solution)/shard_map/ppermute | solution.py:26
  490.7 13.3 %collective-permute-start.4 = (bf16[48,18,2,1]{3,0,2,1:T(8,128)(2,1)S(1)}, bf16[48,18,2,1]{3,0,2,1:T(8,128)(2,1)S(1)}, u32[]{:S(2)}, u32[]{:S(2)}) collective-permute-start(bf16[48,18,2,1]{3,0,2,1:T(8,128)(2,1)S(1)} %get-tuple-element.32), channel_id=1, source_target_pairs={{0,1},{1,2},{2,3},{3,4},{4,5},{5,6},{6,7},{8,9},{9,10},{10,11},{11... | collective-permute-start | bytes 10376 | tf_op jit(solution)/shard_map/ppermute | solution.py:25
  502.5 1.5 copy-start.1
  504.0 0.8 copy-start.2
  533.5 31.4 %copy-start.5 = (pred[8,17]{1,0:T(8,128)(4,1)S(1)}, pred[8,17]{1,0:T(8,128)(4,1)}, u32[]{:S(2)}) copy-start(pred[8,17]{1,0:T(8,128)(4,1)} %constant.46) | copy-start | bytes 412
  564.9 604.1 %all-reduce.9.cloned.1.call-start = ((), (), s32[]{:S(2)}) async-start(), calls=%async_computation.5 | async-start | bytes 442368 | tf_op jit(solution)/shard_map/psum | solution.py:11
Sparse Core Ops, SparseCore 0:
  565.0 115.7 all-reduce.6
  684.0 484.9 all-reduce.8
